TPU v7x, 1024 devices: a whole 4x4x32 slice. The times are simulated.
1024 devices in a mesh: table: 64 (over z, core), bal: 16 (over x, y).
Axes of the slice: x: 4, y: 4, z: 32, core: 2. Of those that a mesh axis runs over, the one named last changes fastest.
Arguments:
- item_ids: int32 [262144], P(('table', 'bal')), may hold values from 0 to 65535, as said below
- hot_slot: int32 [65536], replicated, may hold values from 0 to 1024, as said below
- hot_rows: bfloat16 [1024, 512], replicated, may hold values from -6 to 6
- cold_rows: bfloat16 [65536, 512], P('table'), may hold values from -6 to 6
- hist_lengths: int32 [2048], replicated, may hold values from 1 to 128
- out_grad: bfloat16 [262144, 512], P(('table', 'bal')), may hold values from -6 to 6
- w_uvqk: bfloat16 [512, 2048], replicated, may hold values from -0.25 to 0.25
- w_out: bfloat16 [512, 512], replicated, may hold values from -0.25 to 0.25
Outputs:
- layer_out: bfloat16 [262144, 512], P(('table', 'bal'))
- grad_uvqk: float32 [32768, 2048], P(('table', 'bal'))
- grad_out_proj: float32 [32768, 512], P(('table', 'bal'))
Inputs may be any that keep to these rules, and one draw needn't show every extreme that they name: `item_ids`: item i lies in table shard i // 1024. In each device's block of 256 token slots at most 4 tokens with cold items name items of one shard, and some shard gets exactly 4 of them in every block. `hot_slot`: each value below 1024 is taken by exactly one item; 1024 marks a cold item.
All inputs are finite; a program needn't handle non-finite values.
Results may differ from a plain program's by a relative error of at most 0.012.
Values may be sent and summed in bfloat16 or wider, within the bound.
A program may use at most 64 MiB of HBM per device.

v0:
```python
import math

import jax
import jax.numpy as jnp
from jax import lax
from jax.sharding import PartitionSpec as P

HEADS = 4
MAXLEN = 128
TILE = 64


def side_by_side(arrays, axis, dim, along):
    both = jnp.concatenate(arrays, axis=along)
    whole, at, done = (lax.psum_scatter(both, axis, scatter_dimension=dim, tiled=True), 0, [])
    for a in arrays:
        done.append(lax.slice_in_dim(whole, at, at + a.shape[along], axis=along))
        at += a.shape[along]
    return tuple(done)


def norm_rows(values_in):
    average = jnp.mean(values_in, axis=-1, keepdims=True)
    centred = values_in - average
    spread = jnp.mean(centred * centred, axis=-1, keepdims=True)
    return centred * lax.rsqrt(spread + 1e-05)


def attend(hidden, length):
    row_count = hidden.shape[0]
    features = hidden.shape[1] // 4
    head_size = features // HEADS
    activated = jax.nn.silu(hidden)
    gate_part = activated[:, :features].astype(jnp.bfloat16)
    value_part = activated[:, features : 2 * features].astype(jnp.bfloat16)
    query_part = activated[:, 2 * features : 3 * features].astype(jnp.bfloat16)
    key_part = activated[:, 3 * features :].astype(jnp.bfloat16)
    query_heads = query_part.reshape(row_count, HEADS, head_size)
    key_heads = key_part.reshape(row_count, HEADS, head_size)
    value_heads = value_part.reshape(row_count, HEADS, head_size)
    scores = jnp.einsum(
        "ihe,jhe->hij", query_heads, key_heads, preferred_element_type=jnp.float32
    ) * (1.0 / math.sqrt(head_size))
    position = jnp.arange(row_count, dtype=jnp.int32)
    allowed = (position[None, :] <= position[:, None]) & (position[:, None] < length)
    weights = jnp.where(allowed[None], jax.nn.silu(scores), 0.0).astype(jnp.bfloat16)
    mixed = jnp.einsum(
        "hij,jhe->ihe", weights, value_heads, preferred_element_type=jnp.float32
    ).reshape(row_count, features)
    return (norm_rows(mixed) * gate_part.astype(jnp.float32)).astype(jnp.bfloat16)


def user_pass(user_emb, user_cot, length, w_uvqk, w_out, grad_scale):
    row_count = user_emb.shape[0]
    normed = norm_rows(user_emb.astype(jnp.float32)).astype(jnp.bfloat16)
    hidden = jnp.dot(normed, w_uvqk, preferred_element_type=jnp.float32)
    gated, pullback = jax.vjp(lambda hidden_in: attend(hidden_in, length), hidden)
    output = (
        user_emb.astype(jnp.float32) + jnp.dot(gated, w_out, preferred_element_type=jnp.float32)
    ).astype(jnp.bfloat16)
    is_valid = jnp.arange(row_count, dtype=jnp.int32) < length
    signal = (jnp.where(is_valid[:, None], user_cot.astype(jnp.float32), 0.0) * grad_scale).astype(
        jnp.bfloat16
    )
    back_signal = jnp.dot(signal, w_out.T, preferred_element_type=jnp.float32).astype(jnp.bfloat16)
    grad_hidden = pullback(back_signal)[0].astype(jnp.bfloat16)
    grad_first = jnp.einsum("td,tf->df", normed, grad_hidden, preferred_element_type=jnp.float32)
    grad_second = jnp.einsum("td,tf->df", gated, signal, preferred_element_type=jnp.float32)
    return (output, grad_first, grad_second)


def run_users(emb_stack, cot_stack, len_stack, w_uvqk, w_out, grad_scale):
    features = emb_stack.shape[2]

    def per_user(running, inputs):
        user_emb, user_cot, length = inputs

        def short_pass():
            output, grad_first, grad_second = user_pass(
                user_emb[:TILE], user_cot[:TILE], length, w_uvqk, w_out, grad_scale
            )
            return (jnp.concatenate([output, user_emb[TILE:]], axis=0), grad_first, grad_second)

        def long_pass():
            return user_pass(user_emb, user_cot, length, w_uvqk, w_out, grad_scale)

        output, grad_first, grad_second = lax.cond(length <= TILE, short_pass, long_pass)
        return ((running[0] + grad_first, running[1] + grad_second), output)

    initial = (
        jnp.zeros((features, 4 * features), jnp.float32),
        jnp.zeros((features, features), jnp.float32),
    )
    return lax.scan(per_user, initial, (emb_stack, cot_stack, len_stack))


def per_device(item_ids, hot_slot, hot_rows, cold_rows, hist_lengths, out_grad, w_uvqk, w_out):
    owners = lax.axis_size("table")
    token_count = item_ids.shape[0]
    shard_rows = cold_rows.shape[0]
    hot_count = hot_rows.shape[0]
    capacity = token_count // owners
    hot_index = jnp.take(hot_slot, item_ids)
    is_hot = hot_index < hot_count
    owner_of = item_ids // shard_rows
    shard_row = item_ids % shard_rows
    owner_marks = (
        (owner_of[:, None] == jnp.arange(owners, dtype=jnp.int32)[None, :])
        & jnp.logical_not(is_hot)[:, None]
    ).astype(jnp.int32)
    earlier = jnp.cumsum(owner_marks, axis=0) - owner_marks
    position = jnp.sum(earlier * owner_marks, axis=1)
    target = jnp.where(is_hot, owners, owner_of)
    requests = (
        jnp.zeros((owners, capacity), jnp.int32).at[target, position].set(shard_row, mode="drop")
    )
    found_rows = jnp.take(
        cold_rows,
        lax.all_to_all(requests, "table", split_axis=0, concat_axis=0, tiled=True),
        axis=0,
    )
    replies = lax.all_to_all(found_rows, "table", split_axis=0, concat_axis=0, tiled=True)
    cold_part = replies[owner_of, jnp.minimum(position, capacity - 1)]
    hot_part = jnp.take(hot_rows, jnp.minimum(hot_index, hot_count - 1), axis=0)
    embedded = jnp.where(is_hot[:, None], hot_part, cold_part)
    seq_len = MAXLEN
    user_count = token_count // seq_len
    features = embedded.shape[1]
    bal_count = lax.axis_size("bal")
    bal_index = lax.axis_index("bal")
    user_start = (lax.axis_index("table") * bal_count + bal_index) * user_count
    grad_scale = 1.0 / math.sqrt(bal_count * token_count)
    own_lengths = lax.dynamic_slice_in_dim(hist_lengths, user_start, user_count)
    own_emb = embedded.reshape(user_count, seq_len, features)
    own_cot = out_grad.reshape(user_count, seq_len, features)
    totals, outputs = run_users(own_emb, own_cot, own_lengths, w_uvqk, w_out, grad_scale)
    layer_out = outputs.reshape(token_count, features)
    grad_first, grad_second = side_by_side((totals[0], totals[1]), "bal", 0, 1)
    return (layer_out, grad_first, grad_second)


def solution(mesh):
    return jax.shard_map(
        per_device,
        mesh=mesh,
        in_specs=(
            P(("table", "bal")),
            P(),
            P(),
            P("table", None),
            P(),
            P(("table", "bal"), None),
            P(),
            P(),
        ),
        out_specs=(P(("table", "bal"), None), P(("table", "bal"), None), P(("table", "bal"), None)),
        check_vma=False,
    )
```

profile of v0, /device:TPU:6, one launch (start us, length us, event | category | flops | bytes accessed | tf_op | source)
XLA Modules:
  0.0 290.5 jit_solution(6422404877156455545)
XLA Ops:
  7.2 0.8 and_select_fusion
  8.0 2.2 gather_fusion
  10.2 0.7 and_bitcast_fusion
  11.0 0.6 reduce-window.6
  11.6 0.2 slice_reduce_fusion
  12.0 11.3 %scatter_fusion = s32[64,4]{0,1:T(4,128)S(1)} fusion(s32[64,4]{0,1:T(4,128)S(1)} %broadcast_in_dim.170, s32[256]{0:T(256)S(1)} %bitcast.192, s32[256]{0:T(256)S(1)} %get-tuple-element.184), kind=kCustom, calls=%fused_computation.4 | custom fusion | bytes 5120 | tf_op jit(solution)/shard_map/scatter | solution.py:115
  23.4 52.7 %all_to_all.20 = s32[64,1,4]{2,1,0:T(1,128)S(1)} all-to-all(s32[64,1,4]{2,1,0:T(1,128)S(1)} %copy.91), channel_id=1, replica_groups=mesh['table'=64,'bal'=16] {'table'}, dimensions={0} | all-to-all | bytes 2048 | tf_op jit(solution)/shard_map/all_to_all | solution.py:119
  76.2 1.2 gather_fusion.2
  77.7 0.9 broadcast_select_fusion
  78.6 4.6 %all-to-all-start.1 = ((bf16[64,4,512]{2,1,0:T(4,128)(2,1)}), bf16[64,4,512]{2,1,0:T(4,128)(2,1)S(1)}, u32[]{:S(2)}, u32[]{:S(2)}) async-start(bf16[64,4,512]{2,1,0:T(4,128)(2,1)} %broadcast_select_fusion), calls=%async_computation.1 | async-start | bytes 524288 | tf_op jit(solution)/shard_map/all_to_all | solution.py:122
  83.2 0.2 reduce-scatter.2.cloned.1.call-start
  83.5 1.2 gather_fusion.1
  84.7 0.8 dynamic_slice.14
  85.4 41.1 %all-to-all-done.1 = bf16[64,4,512]{2,1,0:T(4,128)(2,1)S(1)} async-done(((bf16[64,4,512]{2,1,0:T(4,128)(2,1)}), bf16[64,4,512]{2,1,0:T(4,128)(2,1)S(1)}, u32[]{:S(2)}, u32[]{:S(2)}) %all-to-all-start.1) | async-done | bytes 262176 | tf_op jit(solution)/shard_map/all_to_all | solution.py:122
  126.5 2.1 gather_fusion.3
  128.6 0.8 select_select_fusion
  129.4 44.1 %while.15 = (s32[]{:T(128)}, f32[512,2048]{1,0:T(8,128)}, f32[512,512]{1,0:T(8,128)}, bf16[2,128,512]{2,1,0:T(8,128)(2,1)}, s32[2]{0:T(128)S(1)}, /*index=5*/bf1...) while((s32[]{:T(128)}, f32[512,2048]{1,0:T(8,128)}, ...), condition=%wide.region_19.20_spmd.clone, body=%wide.region_4.19_spmd.clone.sunk | while | flops 852329344 | bytes 48458384 | solution.py:94
  129.4 1.0 dynamic-slice_bitcast_fusion.3
  130.4 0.6 dynamic_slice.23
  131.6 14.7 %conditional.3 = (f32[512,2048]{1,0:T(8,128)}, f32[512,512]{1,0:T(8,128)S(1)}, bf16[1,128,512]{2,1,0:T(8,128)(2,1)S(1)}) conditional(s32[]{:T(128)} %convert_element_type.322, (bf16[128,512]{1,0:T(8,128)(2,1)S(1)}, s32[]{:T(128)}, bf16[128,512]{1,0:T(8,128)(2,1)S(1)}, bf16[512,512]{1,0:T(8,128)(2,1)S(1)}, bf16[512,2048]{1,0:T(8,128)(2,1)}) %tuple.81, ...), branch_computations={%region_5.11_spmd, %region_12.18_spmd} | conditional | flops 849707904 | bytes 21457120 | solution.py:87
  131.7 0.2 fusion.17
  131.9 3.1 %multiply_convert_fusion = (bf16[128,2048]{1,0:T(8,128)(2,1)S(1)}, f32[128,2048]{1,0:T(8,128)}) fusion(bf16[512,2048]{1,0:T(8,128)(2,1)} %get-tuple-element.61, bf16[128,512]{1,0:T(8,128)(2,1)S(1)} %get-tuple-element.57, f32[128]{0:T(128)S(1)} %add_rsqrt_fusion, f32[128]{0:T(128)S(1)} %broadcast_multiply_fusion.1), kind=kOutput, calls=%fused_computation.21 | convolution fusion | flops 270008320 | bytes 3802112 | tf_op jit(solution)/shard_map/while/body/eval_jaxpr/cond/branch_0_fun/dot_general | solution.py:56
  135.3 0.2 convolution_multiply_fusion
  135.6 0.6 iota_compare_fusion.1
  136.2 0.3 fusion.112
  136.7 0.7 fusion.24
  137.5 1.0 multiply_reduce_fusion
  138.5 0.7 multiply_multiply_fusion
  139.2 0.9 fusion.108
  140.3 0.3 fusion.22
  140.6 0.2 fusion.115
  140.9 0.2 fusion.114
  141.2 0.2 convolution_convert_fusion
  141.6 4.0 %fusion.8 = f32[512,2048]{1,0:T(8,128)} fusion(f32[128,2048]{1,0:T(8,128)} %get-tuple-element.158, bf16[128,512]{1,0:T(8,128)(2,1)S(1)} %get-tuple-element.151, bf16[128,512]{1,0:T(8,128)(2,1)S(1)} %copy.101, bf16[128,512]{1,0:T(8,128)(2,1)S(1)} %copy.100, bf16[128,512]{1,0:T(8,128)(2,1)S(1)} %copy.99, bf16[128,512]{1,0:T(8,128)(2,1)S(1)} %get-tuple-element.57, ...), kind=kOutput, calls=%fused_computation.23 | convolution fusion | flops 273154048 | bytes 5899264 | tf_op jit(solution)/shard_map/while/body/eval_jaxpr/cond/branch_0_fun/td,tf->df/dot_general | solution.py:67
  145.6 0.4 fusion.31
  146.0 0.2 fusion.4
  146.3 5.5 %select_add_fusion.4 = f32[512,2048]{1,0:T(8,128)} fusion(f32[512,2048]{1,0:T(8,128)} %get-tuple-element.250, f32[512,2048]{1,0:T(8,128)} %get-tuple-element.272, pred[]{:T(512)S(6)} %compare.20), kind=kLoop, calls=%fused_computation.167.clone.1 | loop fusion | flops 2097152 | bytes 12582913 | tf_op jit(solution)/shard_map/while/body/eval_jaxpr/add | solution.py:88
  151.8 0.4 select_add_fusion.5
  152.2 1.0 copy-done.3
  153.2 0.7 copy-done.11
  153.9 1.0 dynamic-slice_bitcast_fusion.3
  154.8 0.6 dynamic_slice.23
  156.0 8.7 %conditional.3 = (f32[512,2048]{1,0:T(8,128)}, f32[512,512]{1,0:T(8,128)S(1)}, bf16[1,128,512]{2,1,0:T(8,128)(2,1)S(1)}) conditional(s32[]{:T(128)} %convert_element_type.322, (bf16[128,512]{1,0:T(8,128)(2,1)S(1)}, s32[]{:T(128)}, bf16[128,512]{1,0:T(8,128)(2,1)S(1)}, bf16[512,512]{1,0:T(8,128)(2,1)S(1)}, bf16[512,2048]{1,0:T(8,128)(2,1)}) %tuple.81, ...), branch_computations={%region_5.11_spmd, %region_12.18_spmd} | conditional | flops 849707904 | bytes 21457120 | solution.py:87
  156.1 0.2 fusion.61
  156.3 2.2 multiply_convert_fusion.5
  158.6 0.6 iota_compare_fusion.3
  159.3 0.3 fusion.113
  159.6 0.2 fusion.68
  159.8 0.4 multiply_reduce_fusion.1
  160.2 0.2 fusion.109
  160.4 0.2 fusion.66
  160.7 0.2 fusion.46
  161.0 0.2 fusion.48
  161.3 2.7 fusion.52
  164.0 0.3 fusion.85
  164.4 0.2 fusion.42
  164.7 6.8 %select_add_fusion.4 = f32[512,2048]{1,0:T(8,128)} fusion(f32[512,2048]{1,0:T(8,128)} %get-tuple-element.250, f32[512,2048]{1,0:T(8,128)} %get-tuple-element.272, pred[]{:T(512)S(6)} %compare.20), kind=kLoop, calls=%fused_computation.167.clone.1 | loop fusion | flops 2097152 | bytes 12582913 | tf_op jit(solution)/shard_map/while/body/eval_jaxpr/add | solution.py:88
  171.5 0.4 select_add_fusion.5
  171.8 1.0 copy-done.3
  172.8 0.7 copy-done.11
  173.5 5.3 %pad_maximum_fusion = f32[512,2560]{1,0:T(8,128)} fusion(f32[512,512]{1,0:T(8,128)} %get-tuple-element.88, f32[512,2048]{1,0:T(8,128)} %get-tuple-element.87), kind=kLoop, calls=%fused_computation.172 | loop fusion | flops 1310720 | bytes 10485760 | tf_op jit(solution)/shard_map/concatenate | solution.py:14
  178.8 101.7 %reduce-scatter.2.cloned.1.call-done = f32[32,2560]{1,0:T(8,128)} async-done(((f32[512,2560]{1,0:T(8,128)}), f32[32,2560]{1,0:T(8,128)}) %reduce-scatter.2.cloned.1.call-update) | async-done | bytes 327696 | tf_op jit(solution)/shard_map/reduce_scatter | solution.py:15
  280.6 1.7 slice.76
  282.2 1.5 slice.77
  (93 shorter events, 2.7 us)
Async XLA Ops:
  7.2 69.1 %copy-start = (bf16[1024,512]{1,0:T(8,128)(2,1)S(1)}, bf16[1024,512]{1,0:T(8,128)(2,1)}, u32[]{:S(2)}) copy-start(bf16[1024,512]{1,0:T(8,128)(2,1)} %param.15) | copy-start | bytes 3145732
  7.2 76.3 %copy-start.4 = (bf16[1024,512]{1,0:T(8,128)(2,1)S(1)}, bf16[1024,512]{1,0:T(8,128)(2,1)}, u32[]{:S(2)}) copy-start(bf16[1024,512]{1,0:T(8,128)(2,1)} %param.14) | copy-start | bytes 3145732
  77.4 52.1 %copy-start.1 = (bf16[512,512]{1,0:T(8,128)(2,1)S(1)}, bf16[512,512]{1,0:T(8,128)(2,1)}, u32[]{:S(2)}) copy-start(bf16[512,512]{1,0:T(8,128)(2,1)} %param.19) | copy-start | bytes 1572868
  78.6 47.9 %all-to-all-start.1 = ((bf16[64,4,512]{2,1,0:T(4,128)(2,1)}), bf16[64,4,512]{2,1,0:T(4,128)(2,1)S(1)}, u32[]{:S(2)}, u32[]{:S(2)}) async-start(bf16[64,4,512]{2,1,0:T(4,128)(2,1)} %broadcast_select_fusion), calls=%async_computation.1 | async-start | bytes 524288 | tf_op jit(solution)/shard_map/all_to_all | solution.py:122
  83.2 197.3 %reduce-scatter.2.cloned.1.call-start = ((), (), s32[]{:S(2)}) async-start(), calls=%async_computation.3 | async-start | bytes 5570560 | tf_op jit(solution)/shard_map/reduce_scatter | solution.py:15
  129.4 2.1 copy-start.12
  131.7 3.3 %copy-start.8 = (f32[128]{0:T(128)}, f32[128]{0:T(128)S(1)}, u32[]{:S(2)}) copy-start(f32[128]{0:T(128)S(1)} %broadcast_multiply_fusion.1) | copy-start | bytes 1540 | tf_op jit(solution)/shard_map/while/body/eval_jaxpr/cond
  131.9 3.6 %copy-start.14 = (f32[128]{0:T(128)}, f32[128]{0:T(128)S(1)}, u32[]{:S(2)}) copy-start(f32[128]{0:T(128)S(1)} %add_rsqrt_fusion) | copy-start | bytes 1540 | tf_op jit(solution)/shard_map/while/body/eval_jaxpr/cond
  136.1 0.5 copy-start.6
  136.7 0.7 copy-start.5
  140.1 1.5 copy-start.9
  140.1 1.5 copy-start.15
  141.4 4.2 %copy-start.7 = (pred[128]{0:T(512)(128)(4,1)S(1)}, pred[128]{0:T(512)(128)(4,1)}, u32[]{:S(2)}) copy-start(pred[128]{0:T(512)(128)(4,1)} %copy-done.6) | copy-start | bytes 388 | tf_op jit(solution)/shard_map/while/body/eval_jaxpr/cond
  146.2 5.5 %copy-start.2 = (f32[512,512]{1,0:T(8,128)S(1)}, f32[512,512]{1,0:T(8,128)}, u32[]{:S(2)}) copy-start(f32[512,512]{1,0:T(8,128)} %get-tuple-element.273) | copy-start | bytes 3145732 | tf_op jit(solution)/shard_map/while
  146.2 6.9 %copy-start.10 = (bf16[2,128,512]{2,1,0:T(8,128)(2,1)S(1)}, bf16[2,128,512]{2,1,0:T(8,128)(2,1)}, u32[]{:S(2)}) copy-start(bf16[2,128,512]{2,1,0:T(8,128)(2,1)} %get-tuple-element.274) | copy-start | bytes 786436 | tf_op jit(solution)/shard_map/while
  146.3 7.6 %copy-start.13 = (s32[2]{0:T(128)S(1)}, s32[2]{0:T(128)}, u32[]{:S(2)}) copy-start(s32[2]{0:T(128)} %copy-done.12) | copy-start | bytes 28 | tf_op jit(solution)/shard_map/while
  152.1 1.0 copy-start.3
  153.1 0.7 copy-start.11
  153.9 2.1 copy-start.12
  164.7 6.8 %copy-start.2 = (f32[512,512]{1,0:T(8,128)S(1)}, f32[512,512]{1,0:T(8,128)}, u32[]{:S(2)}) copy-start(f32[512,512]{1,0:T(8,128)} %get-tuple-element.273) | copy-start | bytes 3145732 | tf_op jit(solution)/shard_map/while
  164.7 8.1 %copy-start.10 = (bf16[2,128,512]{2,1,0:T(8,128)(2,1)S(1)}, bf16[2,128,512]{2,1,0:T(8,128)(2,1)}, u32[]{:S(2)}) copy-start(bf16[2,128,512]{2,1,0:T(8,128)(2,1)} %get-tuple-element.274) | copy-start | bytes 786436 | tf_op jit(solution)/shard_map/while
  164.7 8.9 %copy-start.13 = (s32[2]{0:T(128)S(1)}, s32[2]{0:T(128)}, u32[]{:S(2)}) copy-start(s32[2]{0:T(128)} %copy-done.12) | copy-start | bytes 28 | tf_op jit(solution)/shard_map/while
  171.8 1.0 copy-start.3
  172.8 0.7 copy-start.11
Sparse Core Ops, SparseCore 0:
  178.9 101.5 reduce-scatter.1
where the time goes:
time: 291 us
  waiting for transfers between devices  143 us (49%)
  blocking collectives  52.7 us (18%)
  local copies, waits for them, and re-layouts  30.1 us (10%)
  other arithmetic  27 us (9%)
  matrix products  17.2 us (6%)
  between operations  14.2 us (5%)
  starting transfers between devices  4.85 us (2%)
    reduce_scatter x1, waiting for transfers between devices, side_by_side(): lax.psum_scatter(both, axis, scatter_dimension=dim, tiled=True)  102 us
    all_to_all x1, blocking collectives, per_device(): lax.all_to_all(requests, 'table', split_axis=0, concat_axis=0, tiled=True)  52.7 us
    all_to_all x1, waiting for transfers between devices, per_device(): lax.all_to_all(found_rows, 'table', split_axis=0, concat_axis=0, tiled=True)  41.1 us
    add x4, other arithmetic, per_user(): return ((running[0] + grad_first, running[1] + grad_second), output)  13 us
    scatter x1, local copies, waits for them, and re-layouts, per_device(): jnp.zeros((owners, capacity), jnp.int32).at[target, position]  11.3 us
    dot_general x2, matrix products, user_pass(): jnp.einsum('td,tf->df', normed, grad_hidden, preferred_element_type=jnp.f...  6.78 us
  transfers between devices with their start and end apart: 2, of which 2 were waited for; matrix products, arithmetic and copies ran while one was open for 1% of the time, Pallas kernels for 0%

commit v1 on v0

v1 whole, which is shorter than its diff:
```python
import functools
import math

import jax
import jax.numpy as jnp
from jax import lax
from jax.experimental import pallas as pl
from jax.experimental.pallas import tpu as pltpu
from jax.sharding import PartitionSpec as P

HEADS = 4
MAXLEN = 128
HALF = 1280
BF, F32 = jnp.bfloat16, jnp.float32
VMEM = pl.BlockSpec(memory_space=pltpu.VMEM)
SMEM = pl.BlockSpec(memory_space=pltpu.SMEM)


def dot(a, b, ca=1, cb=0):
    return lax.dot_general(a, b, (((ca,), (cb,)), ((), ())), preferred_element_type=F32)


def iota(shape, dim):
    return lax.broadcasted_iota(jnp.int32, shape, dim)


def one_hot(cond):
    return jnp.where(cond, 1.0, 0.0).astype(BF)


def each_peer(n, me, do):
    do(lax.rem(me + n // 2, n))

    def both(i, _):
        away = n // 2 - 1 - i
        do(lax.rem(me + away, n))
        do(lax.rem(me + n - away, n))
        return 0

    lax.fori_loop(0, n // 2 - 1, both, 0)


def lookup_kernel(
    n, ids_ref, slot_ref, hot_ref, cold_ref, emb_ref,
    ask, asked, wide, found, reply, barely, send_sem, recv_sem,
):
    me = lax.axis_index("table")
    barrier = pltpu.get_barrier_semaphore()

    def greet(peer):
        pl.semaphore_signal(barrier, inc=1, device_id={"table": peer}, device_id_type=pl.DeviceIdType.MESH)

    each_peer(n, me, greet)

    tokens = ids_ref.shape[1]
    per = tokens // n
    shard = cold_ref.shape[0]
    hot_count = hot_ref.shape[0]
    ids_row = jnp.broadcast_to(ids_ref[...].astype(F32), (tokens, tokens))
    diag = iota((tokens, tokens), 0) == iota((tokens, tokens), 1)
    ids = jnp.sum(jnp.where(diag, ids_row, 0.0), axis=1, keepdims=True).astype(jnp.int32)
    lines = slot_ref.shape[0]
    pick = one_hot(iota((tokens, lines), 1) == ids // 128)
    slots = slot_ref[...]
    high = dot(pick, (slots // 8).astype(F32).astype(BF))
    low = dot(pick, (slots % 8).astype(F32).astype(BF))
    lane = iota((tokens, 128), 1)
    hot_index = jnp.sum(jnp.where(lane == ids % 128, high * 8.0 + low, 0.0), axis=1, keepdims=True).astype(jnp.int32)
    owner = ids // shard
    row = ids % shard
    cold = hot_index >= hot_count
    marks = one_hot((lane == owner) & cold)
    before = dot(one_hot(iota((tokens, tokens), 1) < iota((tokens, tokens), 0)), marks)
    place = jnp.sum(before * marks.astype(F32), axis=1, keepdims=True).astype(jnp.int32)
    digits = jnp.where(
        lane == place, (row // 8).astype(F32), jnp.where(lane == place + per, (row % 8).astype(F32), 0.0)
    ).astype(BF)
    ask[...] = dot(marks, digits, 0, 0)[:n].reshape(n, 1, 128)

    pl.semaphore_wait(barrier, n - 1)

    def send(src, dst, k):
        def one(peer):
            pltpu.make_async_remote_copy(
                src_ref=src.at[peer], dst_ref=dst.at[me], send_sem=send_sem.at[k], recv_sem=recv_sem.at[k],
                device_id={"table": peer}, device_id_type=pl.DeviceIdType.MESH,
            ).start()

        each_peer(n, me, one)

    def settle(ref, sem):
        part = ref.at[pl.ds(0, n - 1)]
        pltpu.make_async_copy(part, part, sem).wait()

    send(ask, asked, 0)
    asked[me] = ask[me]
    hot_part = dot(one_hot(iota((tokens, hot_count), 1) == hot_index), hot_ref[...])
    settle(asked, recv_sem.at[0])

    spread = one_hot(iota((tokens, n), 0) // per == iota((tokens, n), 1))
    got = dot(spread, asked[...].reshape(n, 128).astype(BF))
    turn = iota((tokens, 128), 0) % per
    want = jnp.sum(
        jnp.where(lane == turn, got * 8.0, jnp.where(lane == turn + per, got, 0.0)), axis=1, keepdims=True
    ).astype(jnp.int32)
    rows = dot(one_hot(iota((tokens, shard), 1) == want), cold_ref[...])
    pieces = rows.shape[1] // 128
    for j in range(pieces):
        wide[pl.ds(j, tokens, stride=pieces), :] = rows[:, j * 128 : (j + 1) * 128]
    found[...] = wide[...].astype(BF).reshape(found.shape)
    send(found, reply, 1)
    reply[me] = found[me]
    barely[...] = hot_part
    slot = jnp.where(cold, owner * per + place, -1)
    settle(reply, recv_sem.at[1])

    wide[...] = reply[...].reshape(wide.shape).astype(F32)
    take = one_hot(iota((tokens, tokens), 1) == slot)
    for j in range(pieces):
        cut = slice(j * 128, (j + 1) * 128)
        piece = wide[pl.ds(j, tokens, stride=pieces), :].astype(BF)
        emb_ref[:, cut] = (barely[:, cut] + dot(take, piece)).astype(BF)
    settle(ask, send_sem.at[0])
    settle(found, send_sem.at[1])


def lookup(n, ids, hot_slot, hot_rows, cold_rows):
    tokens = ids.shape[0]
    features = hot_rows.shape[1]
    piece = features // 128 * (tokens // n)
    return pl.pallas_call(
        functools.partial(lookup_kernel, n),
        out_shape=jax.ShapeDtypeStruct((tokens, features), BF),
        in_specs=[VMEM] * 4,
        out_specs=VMEM,
        scratch_shapes=[
            pltpu.VMEM((n, 1, 128), F32),
            pltpu.VMEM((n, 1, 128), F32),
            pltpu.VMEM((n * piece, 128), F32),
            pltpu.VMEM((n, piece, 128), BF),
            pltpu.VMEM((n, piece, 128), BF),
            pltpu.VMEM((tokens, features), F32),
            pltpu.SemaphoreType.DMA((2,)),
            pltpu.SemaphoreType.DMA((2,)),
        ],
        compiler_params=pltpu.CompilerParams(
            collective_id=0, has_side_effects=True, vmem_limit_bytes=40 * 2**20
        ),
        name="lookup",
    )(ids.reshape(1, tokens), hot_slot.reshape(-1, 128), hot_rows, cold_rows)


def normalised(values):
    mean = jnp.mean(values, axis=-1, keepdims=True)
    centred = values - mean
    scale = lax.rsqrt(jnp.mean(centred * centred, axis=-1, keepdims=True) + 1e-05)
    return centred * scale, scale


def silu_both(v):
    sig = 0.5 * jnp.tanh(0.5 * v) + 0.5
    act = v * sig
    return act, sig + act * (1.0 - sig)


def layer_kernel(
    grad_scale, len_ref, emb_ref, cot_ref, wu_ref, wo_ref, out_ref, grad_ref,
    slope, acts, attn, attn_slope, mixed, grads,
):
    tokens, features = emb_ref.shape
    users = tokens // MAXLEN
    head = features // HEADS
    first = (lax.axis_index("table") * lax.axis_size("bal") + lax.axis_index("bal")) * users
    lengths = [len_ref[first + u] for u in range(users)]
    emb = emb_ref[...].astype(F32)
    normed = normalised(emb)[0].astype(BF)
    for b in range(4):
        cut = slice(b * features, (b + 1) * features)
        act, dact = silu_both(dot(normed, wu_ref[:, cut]))
        acts[:, cut] = act.astype(BF)
        slope[:, cut] = dact
    i, j = iota((MAXLEN, MAXLEN), 0), iota((MAXLEN, MAXLEN), 1)
    scale = 1.0 / math.sqrt(head)

    def part(b, u, h):
        at = b * features + h * head
        return acts[u * MAXLEN : (u + 1) * MAXLEN, at : at + head]

    for u in range(users):
        allowed = (j <= i) & (i < lengths[u])
        for h in range(HEADS):
            s = dot(part(2, u, h), part(3, u, h), 1, 1) * scale
            act, dact = silu_both(s)
            w = jnp.where(allowed, act, 0.0).astype(BF)
            attn[u * HEADS + h] = w
            attn_slope[u * HEADS + h] = jnp.where(allowed, dact * scale, 0.0)
            mixed[u * MAXLEN : (u + 1) * MAXLEN, h * head : (h + 1) * head] = dot(w, part(1, u, h))

    n, rstd = normalised(mixed[...])
    gate = acts[:, :features].astype(F32)
    gated = (n * gate).astype(BF)
    out_ref[...] = (emb + dot(gated, wo_ref[...])).astype(BF)
    at = iota((tokens, 1), 0)
    ends = jnp.full((tokens, 1), lengths[0], jnp.int32)
    for u in range(1, users):
        ends = jnp.where(at >= u * MAXLEN, u * MAXLEN + lengths[u], ends)
    valid = at < ends
    signal = (jnp.where(valid, cot_ref[...].astype(F32), 0.0) * grad_scale).astype(BF)
    back = dot(signal, wo_ref[...], 1, 1).astype(BF).astype(F32)
    dn = back * gate
    dmixed = rstd * (
        dn - jnp.mean(dn, axis=-1, keepdims=True) - n * jnp.mean(dn * n, axis=-1, keepdims=True)
    )
    mixed[...] = dmixed
    grads[:, :features] = ((back * n).astype(BF).astype(F32) * slope[:, :features]).astype(BF)
    for u in range(users):
        rows = slice(u * MAXLEN, (u + 1) * MAXLEN)
        for h in range(HEADS):
            dm = mixed[rows, h * head : (h + 1) * head].astype(BF)
            w = attn[u * HEADS + h]
            dw = dot(dm, part(1, u, h), 1, 1).astype(BF).astype(F32)
            ds = (dw * attn_slope[u * HEADS + h]).astype(BF)
            for b, d in (
                (1, dot(w, dm, 0, 0)),
                (2, dot(ds, part(3, u, h))),
                (3, dot(ds, part(2, u, h), 0, 0)),
            ):
                cols = slice(b * features + h * head, b * features + (h + 1) * head)
                grads[rows, cols] = (d.astype(BF).astype(F32) * slope[rows, cols]).astype(BF)

    across = 256
    height = features // 16
    for c in range(0, 4 * features, across):
        emit(grad_ref, dot(normed, grads[:, c : c + across], 0, 0).astype(BF), c, height)
    for c in range(0, features, across):
        emit(grad_ref, dot(gated, signal[:, c : c + across], 0, 0).astype(BF), 4 * features + c, height)


def emit(grad_ref, value, column, height):
    half, at = divmod(column, HALF)
    for b in range(16):
        x, y = divmod(b, 4)
        f, s = (x, y) if half == 0 else (y, x)
        grad_ref[half, f, s, :, at : at + value.shape[1]] = value[b * height : (b + 1) * height]


def layer(grad_scale, lengths, emb, cot, wu, wo):
    tokens, features = emb.shape
    users = tokens // MAXLEN
    return pl.pallas_call(
        functools.partial(layer_kernel, grad_scale),
        out_shape=(
            jax.ShapeDtypeStruct((tokens, features), BF),
            jax.ShapeDtypeStruct((2, 4, 4, features // 16, HALF), BF),
        ),
        in_specs=[SMEM] + [VMEM] * 4,
        out_specs=(VMEM, VMEM),
        scratch_shapes=[
            pltpu.VMEM((tokens, 4 * features), F32),
            pltpu.VMEM((tokens, 4 * features), BF),
            pltpu.VMEM((users * HEADS, MAXLEN, MAXLEN), BF),
            pltpu.VMEM((users * HEADS, MAXLEN, MAXLEN), F32),
            pltpu.VMEM((tokens, features), F32),
            pltpu.VMEM((tokens, 4 * features), BF),
        ],
        compiler_params=pltpu.CompilerParams(vmem_limit_bytes=48 * 2**20),
        name="layer",
    )(lengths, emb, cot, wu, wo)


def reduce_kernel(
    g, first_ref, second_ref, in1, out1, total, tot_bf, in2, out2, send1, recv1, send2, recv2
):
    me = lax.axis_index("bal")
    x, y = me // 4, me % 4

    def along_x(step):
        return (x + step) % 4 * 4 + y

    def along_y(step):
        return x * 4 + (y + step) % 4

    def copy(src, dst, send_sem, recv_sem, peer):
        return pltpu.make_async_remote_copy(
            src_ref=src, dst_ref=dst, send_sem=send_sem, recv_sem=recv_sem,
            device_id={"bal": peer}, device_id_type=pl.DeviceIdType.MESH,
        )

    barrier = pltpu.get_barrier_semaphore()
    for peer in (along_x(1), along_x(3), along_y(1), along_y(3)):
        pl.semaphore_signal(barrier, inc=1, device_id={"bal": peer}, device_id_type=pl.DeviceIdType.MESH)
    pl.semaphore_wait(barrier, 4)

    ways = [(half, way) for half in range(2) for way in range(2)]
    steps = (1, 3)
    places = ((x, y), (y, x))
    moves = ((along_x, along_y), (along_y, along_x))
    copies = []

    def stage1(half, way, msg):
        a = places[half][0]
        mine, other = pl.ds(2 * way, 2), pl.ds(2 - 2 * way, 2)
        src = (
            g.at[half, (a + 2) % 4, mine],
            g.at[half, (a + steps[way]) % 4, other],
            out1.at[half, way],
        )[msg]
        c = copy(
            src, in1.at[half, way, msg], send1.at[half, way, msg], recv1.at[half, way, msg],
            moves[half][0](steps[way]),
        )
        c.start()
        return c

    sent = {}
    for msg in (0, 1):
        for half, way in ways:
            sent[half, way, msg] = stage1(half, way, msg)
    for half, way in ways:
        a = places[half][0]
        sent[half, way, 0].wait_recv()
        own = g[half, (a + steps[way]) % 4, pl.ds(2 * way, 2)]
        out1[half, way] = (own.astype(F32) + in1[half, way, 0].astype(F32)).astype(BF)
        sent[half, way, 2] = stage1(half, way, 2)

    height = first_ref.shape[0]
    mid = height // 2

    def stage2(half, way, msg):
        b = places[half][1]
        mine, other = pl.ds(mid * way, mid), pl.ds(mid - mid * way, mid)
        src = (
            tot_bf.at[half, (b + 2) % 4, mine],
            tot_bf.at[half, (b + steps[way]) % 4, other],
            out2.at[half, way],
        )[msg]
        c = copy(
            src, in2.at[half, way, msg], send2.at[half, way, msg], recv2.at[half, way, msg],
            moves[half][1](steps[way]),
        )
        c.start()
        return c

    later = {}
    for half in range(2):
        a = places[half][0]
        for way in range(2):
            sent[half, way, 1].wait_recv()
            sent[half, way, 2].wait_recv()
        for part in range(2):
            here = pl.ds(2 * part, 2)
            t = (
                g[half, a, here].astype(F32)
                + in1[half, part, 2].astype(F32)
                + in1[half, 1 - part, 1].astype(F32)
            )
            total[half, here] = t
            tot_bf[half, here] = t.astype(BF)
        for msg in (0, 1):
            for way in range(2):
                later[half, way, msg] = stage2(half, way, msg)
    for half, way in ways:
        b = places[half][1]
        later[half, way, 0].wait_recv()
        own = total[half, (b + steps[way]) % 4, pl.ds(mid * way, mid)]
        out2[half, way] = (own + in2[half, way, 0].astype(F32)).astype(BF)
        later[half, way, 2] = stage2(half, way, 2)
    split = first_ref.shape[1] - HALF
    for half in range(2):
        b = places[half][1]
        for way in range(2):
            later[half, way, 1].wait_recv()
            later[half, way, 2].wait_recv()
        for part in range(2):
            rows = pl.ds(mid * part, mid)
            t = (
                total[half, b, rows]
                + in2[half, part, 2].astype(F32)
                + in2[half, 1 - part, 1].astype(F32)
            )
            if half == 0:
                first_ref[rows, :HALF] = t
            else:
                first_ref[rows, HALF:] = t[:, :split]
                second_ref[rows, :] = t[:, split:]
    for c in (*sent.values(), *later.values()):
        c.wait_send()


def reduce(g, features):
    height = features // 16
    dma = pltpu.SemaphoreType.DMA((2, 2, 3))
    return pl.pallas_call(
        reduce_kernel,
        out_shape=(
            jax.ShapeDtypeStruct((height, 4 * features), F32),
            jax.ShapeDtypeStruct((height, features), F32),
        ),
        in_specs=[VMEM],
        out_specs=(VMEM, VMEM),
        scratch_shapes=[
            pltpu.VMEM((2, 2, 3, 2, height, HALF), BF),
            pltpu.VMEM((2, 2, 2, height, HALF), BF),
            pltpu.VMEM((2, 4, height, HALF), F32),
            pltpu.VMEM((2, 4, height, HALF), BF),
            pltpu.VMEM((2, 2, 3, height // 2, HALF), BF),
            pltpu.VMEM((2, 2, height // 2, HALF), BF),
            dma, dma, dma, dma,
        ],
        compiler_params=pltpu.CompilerParams(
            collective_id=1, has_side_effects=True, vmem_limit_bytes=40 * 2**20
        ),
        name="reduce",
    )(g)


def per_device(item_ids, hot_slot, hot_rows, cold_rows, hist_lengths, out_grad, w_uvqk, w_out):
    tokens, features = out_grad.shape
    grad_scale = 1.0 / math.sqrt(lax.axis_size("bal") * tokens)
    emb = lookup(lax.axis_size("table"), item_ids, hot_slot, hot_rows, cold_rows)
    layer_out, g = layer(grad_scale, hist_lengths, emb, out_grad, w_uvqk, w_out)
    return (layer_out, *reduce(g, features))


def solution(mesh):
    both = P(("table", "bal"), None)
    return jax.shard_map(
        per_device,
        mesh=mesh,
        in_specs=(P(("table", "bal")), P(), P(), P("table", None), P(), both, P(), P()),
        out_specs=(both, both, both),
        check_vma=False,
    )
```

time: 291 us -> 104 us (0.36)
  waiting for transfers between devices: 143 us -> 0 us
  Pallas kernels: 0 us -> 95.2 us
  blocking collectives: 52.7 us -> 0 us
  other arithmetic: 27 us -> 0 us
  local copies, waits for them, and re-layouts: 30.1 us -> 7.2 us
  matrix products: 17.2 us -> 0 us
  between operations: 14.2 us -> 0.7 us
  starting transfers between devices: 4.85 us -> 0 us
    reduce_scatter x1 -> x0, waiting for transfers between devices: 102 us -> none  [side_by_side(): lax.psum_scatter(both, axis, scatter_dimension=dim, tiled=True)]
    pallas_call x0 -> x3, Pallas kernels: none -> 95.2 us  [the longest x1 65.8 us: lookup(): pl.pallas_call(functools.partial(lookup_kernel, n), out_shape=jax.ShapeDt...]
    all_to_all x1 -> x0, blocking collectives: 52.7 us -> none  [per_device(): lax.all_to_all(requests, 'table', split_axis=0, concat_axis=0, tiled=True)]
    all_to_all x1 -> x0, waiting for transfers between devices: 41.1 us -> none  [per_device(): lax.all_to_all(found_rows, 'table', split_axis=0, concat_axis=0, tiled=True)]
    dot_general x22 -> x0, matrix products: 17.2 us -> none  [the longest x2 6.78 us: user_pass(): jnp.einsum('td,tf->df', normed, grad_hidden, preferred_element_type=jnp.f...]
    add x4 -> x0, other arithmetic: 13 us -> none  [per_user(): return ((running[0] + grad_first, running[1] + grad_second), output)]
    scatter x1 -> x0, local copies, waits for them, and re-layouts: 11.3 us -> none  [per_device(): jnp.zeros((owners, capacity), jnp.int32).at[target, position]]
    unnamed x6 -> x18, local copies, waits for them, and re-layouts: 0.02 us -> 7.2 us
  transfers between devices with their start and end apart: 2 -> 0, of which waited for: 2 -> 0; matrix products, arithmetic and copies ran while one was open for 1% -> 0% of each run, Pallas kernels for 0% -> 0%
where the time goes in v1:
time: 104 us; the launch traced here: 103 us
  Pallas kernels  95.2 us (92%)
  local copies, waits for them, and re-layouts  7.2 us (7%)
    pallas_call x1, Pallas kernels, lookup(): pl.pallas_call(functools.partial(lookup_kernel, n), out_shape=jax.ShapeDt...  65.8 us
    pallas_call x1, Pallas kernels, reduce(): pl.pallas_call(reduce_kernel, out_shape=(jax.ShapeDtypeStruct((height, 4...  23.5 us
    unnamed x18, local copies, waits for them, and re-layouts  7.2 us
    pallas_call x1, Pallas kernels, layer(): pl.pallas_call(functools.partial(layer_kernel, grad_scale), out_shape=(ja...  5.88 us

profile of v1, /device:TPU:6, one launch (start us, length us, event | category | flops | bytes accessed | tf_op | source)
XLA Modules:
  0.0 103.1 jit_solution(9922189707276908302)
XLA Ops:
  0.6 0.0 copy-start
  0.6 0.0 copy-start.1
  0.7 1.4 %copy-done.1 = bf16[1024,512]{1,0:T(8,128)(2,1)S(1)} copy-done((bf16[1024,512]{1,0:T(8,128)(2,1)S(1)}, bf16[1024,512]{1,0:T(8,128)(2,1)}, u32[]{:S(2)}) %copy-start.1) | copy-done | bytes 1048600
  2.0 0.0 copy-start.2
  2.0 1.2 %copy-done.2 = bf16[1024,512]{1,0:T(8,128)(2,1)S(1)} copy-done((bf16[1024,512]{1,0:T(8,128)(2,1)S(1)}, bf16[1024,512]{1,0:T(8,128)(2,1)}, u32[]{:S(2)}) %copy-start.2) | copy-done | bytes 1048600
  3.2 0.0 copy-start.4
  3.2 0.9 copy-done.4
  4.2 0.0 copy-start.7
  4.2 0.7 copy-done.7
  4.9 0.0 copy-start.3
  4.9 65.8 %lookup.1.emb_ref = bf16[256,512]{1,0:T(8,128)(2,1)S(1)} custom-call(s32[1,256]{1,0:T(1,128)S(1)} %bitcast.3, s32[512,128]{1,0:T(8,128)S(1)} %bitcast.2, bf16[1024,512]{1,0:T(8,128)(2,1)S(1)} %copy-done.1, bf16[1024,512]{1,0:T(8,128)(2,1)S(1)} %copy-done.2), custom_call_target="tpu_custom_call" | custom-call | tf_op jit(solution)/shard_map/lookup/pallas_call | solution.py:131
  70.7 0.0 copy-done
  70.7 0.0 copy-done.3
  70.7 0.0 copy-start.5
  70.7 0.9 copy-done.5
  71.7 0.0 copy-start.6
  71.7 0.7 copy-done.6
  72.4 5.9 %layer.1 = (bf16[256,512]{1,0:T(8,128)(2,1)}, bf16[2,4,4,32,1280]{4,3,2,1,0:T(8,128)(2,1)S(1)}) custom-call(s32[2048]{0:T(1024)S(1)} %copy-done.6, bf16[256,512]{1,0:T(8,128)(2,1)S(1)} %lookup.1.emb_ref, bf16[256,512]{1,0:T(8,128)(2,1)S(1)} %copy-done.5, bf16[512,2048]{1,0:T(8,128)(2,1)S(1)} %copy-done, bf16[512,512]{1,0:T(8,128)(2,1)S(1)} %copy-done.3), custom_call_target="tpu_custom_call" | custom-call | tf_op jit(solution)/shard_map/layer/pallas_call | solution.py:250
  78.2 23.5 %reduce.1 = (f32[32,2048]{1,0:T(8,128)S(1)}, f32[32,512]{1,0:T(8,128)S(1)}) custom-call(bf16[2,4,4,32,1280]{4,3,2,1,0:T(8,128)(2,1)S(1)} %get-tuple-element.8.g), custom_call_target="tpu_custom_call" | custom-call | tf_op jit(solution)/shard_map/reduce/pallas_call | solution.py:393
  101.8 0.7 copy.13
  102.5 0.6 copy.14
Async XLA Ops:
  0.6 70.1 %copy-start = (bf16[512,2048]{1,0:T(8,128)(2,1)S(1)}, bf16[512,2048]{1,0:T(8,128)(2,1)}, u32[]{:S(2)}) copy-start(bf16[512,2048]{1,0:T(8,128)(2,1)} %wu_ref.1) | copy-start | bytes 6291460
  0.6 1.4 %copy-start.1 = (bf16[1024,512]{1,0:T(8,128)(2,1)S(1)}, bf16[1024,512]{1,0:T(8,128)(2,1)}, u32[]{:S(2)}) copy-start(bf16[1024,512]{1,0:T(8,128)(2,1)} %hot_ref.1) | copy-start | bytes 3145732
  2.0 1.2 %copy-start.2 = (bf16[1024,512]{1,0:T(8,128)(2,1)S(1)}, bf16[1024,512]{1,0:T(8,128)(2,1)}, u32[]{:S(2)}) copy-start(bf16[1024,512]{1,0:T(8,128)(2,1)} %cold_ref.1) | copy-start | bytes 3145732
  3.2 0.9 copy-start.4
  4.2 0.7 copy-start.7
  4.9 65.8 %copy-start.3 = (bf16[512,512]{1,0:T(8,128)(2,1)S(1)}, bf16[512,512]{1,0:T(8,128)(2,1)}, u32[]{:S(2)}) copy-start(bf16[512,512]{1,0:T(8,128)(2,1)} %wo_ref.1) | copy-start | bytes 1572868
  70.7 1.0 copy-start.5
  71.7 0.7 copy-start.6

commit v2 on v0

v2 whole, which is shorter than its diff:
```python
import functools
import math

import jax
import jax.numpy as jnp
from jax import lax
from jax.experimental import pallas as pl
from jax.experimental.pallas import tpu as pltpu
from jax.sharding import PartitionSpec as P

HEADS = 4
MAXLEN = 128
BF, F32 = jnp.bfloat16, jnp.float32
VMEM = pl.BlockSpec(memory_space=pltpu.VMEM)
HBM = pl.BlockSpec(memory_space=pltpu.HBM)


def dot(a, b, ca=1, cb=0):
    return lax.dot_general(a, b, (((ca,), (cb,)), ((), ())), preferred_element_type=F32)


def iota(shape, dim):
    return lax.broadcasted_iota(jnp.int32, shape, dim)


def one_hot(cond):
    return jnp.where(cond, 1.0, 0.0).astype(BF)


def at_distance(z_count, me, d, do):
    z, core = me // 2, me % 2
    for step, rank, mirrored in ((d, 2 * d - 1, 2 * d), (z_count - d, 2 * d, 2 * d - 1)):
        for c in range(2):
            do(lax.rem(z + step, z_count) * 2 + c, rank * 2 + c, mirrored * 2 + core)


def in_range(z_count, me, low, high, do):
    z, core = me // 2, me % 2
    if high == z_count // 2:
        for c in range(2):
            do(lax.rem(z + high, z_count) * 2 + c, (z_count - 1) * 2 + c, (z_count - 1) * 2 + core)
        high -= 1
    least = max(low, 1)

    def one(i, _):
        at_distance(z_count, me, high - i, do)
        return 0

    lax.fori_loop(0, high - least + 1, one, 0)
    if low == 0:
        do(z * 2 + 1 - core, 1 - core, core)


def ranges(z_count):
    ends = [z_count // 8 - 1, z_count // 4 - 1, 3 * z_count // 8 - 1, z_count // 2]
    low, first, out = 0, 0, []
    for high in ends:
        last = 2 * z_count if high == z_count // 2 else 4 * high + 2
        out.append((low, high, first, last))
        low, first = high + 1, last
    return out


def lookup(
    n, loads, near, meanwhile, ids_ref, slot_ref, hot_ref, cold_ref, ask, asked, wide, found, reply, emb_ref,
    ask_send, ask_recv, reply_send, reply_recv,
):
    z_count = n // 2
    me = lax.axis_index("table")
    z, core = me // 2, me % 2
    batches = ranges(z_count)
    barrier = pltpu.get_barrier_semaphore()

    def greet(peer, mine, theirs):
        pl.semaphore_signal(barrier, inc=1, device_id={"table": peer}, device_id_type=pl.DeviceIdType.MESH)

    in_range(z_count, me, 0, z_count // 2, greet)
    for peer in near:
        pl.semaphore_signal(barrier, inc=1, device_id={"bal": peer}, device_id_type=pl.DeviceIdType.MESH)

    tokens = ids_ref.shape[1]
    per = tokens // n
    shard = cold_ref.shape[0]
    hot_count = hot_ref.shape[0]
    loads[6].wait()
    ids_row = jnp.broadcast_to(ids_ref[...].astype(F32), (tokens, tokens))
    diag = iota((tokens, tokens), 0) == iota((tokens, tokens), 1)
    ids = jnp.sum(jnp.where(diag, ids_row, 0.0), axis=1, keepdims=True).astype(jnp.int32)
    lines = slot_ref.shape[0]
    pick = one_hot(iota((tokens, lines), 1) == ids // 128)
    loads[0].wait()
    slots = slot_ref[...]
    high = dot(pick, (slots // 8).astype(F32).astype(BF))
    low = dot(pick, (slots % 8).astype(F32).astype(BF))
    lane = iota((tokens, 128), 1)
    hot_index = jnp.sum(jnp.where(lane == ids % 128, high * 8.0 + low, 0.0), axis=1, keepdims=True).astype(jnp.int32)
    owner = ids // shard
    row = ids % shard
    away = (owner // 2 - z + z_count) % z_count
    rank = jnp.where(away == 0, 0, jnp.where(away <= z_count // 2, 2 * away - 1, 2 * (z_count - away)))
    owner = rank * 2 + owner % 2
    cold = hot_index >= hot_count
    marks = one_hot((lane == owner) & cold)
    before = dot(one_hot(iota((tokens, tokens), 1) < iota((tokens, tokens), 0)), marks)
    place = jnp.sum(before * marks.astype(F32), axis=1, keepdims=True).astype(jnp.int32)
    digits = jnp.where(
        lane == place, (row // 8).astype(F32), jnp.where(lane == place + per, (row % 8).astype(F32), 0.0)
    ).astype(BF)
    ask[...] = dot(marks, digits, 0, 0)[:n].reshape(n, 1, 128)

    pl.semaphore_wait(barrier, n - 1 + len(near))

    def send(src, dst, low, high, out_sem, in_sem):
        def one(peer, mine, theirs):
            pltpu.make_async_remote_copy(
                src_ref=src.at[mine], dst_ref=dst.at[theirs], send_sem=out_sem, recv_sem=in_sem,
                device_id={"table": peer}, device_id_type=pl.DeviceIdType.MESH,
            ).start()

        in_range(z_count, me, low, high, one)

    def settle(ref, first, last, sem):
        part = ref.at[pl.ds(first, last - first)]
        pltpu.make_async_copy(part, part, sem).wait()

    for k, (low_d, high_d, _, _) in reversed(list(enumerate(batches))):
        send(ask, asked, low_d, high_d, ask_send, ask_recv.at[k])
    asked[core] = ask[core]
    loads[2].wait()
    emb_ref[...] = dot(one_hot(iota((tokens, hot_count), 1) == hot_index), hot_ref[...])
    loads[1].wait()

    pieces = cold_ref.shape[1] // 128
    for k, (low_d, high_d, first, last) in enumerate(batches):
        settle(asked, first + (k == 0), last, ask_recv.at[k])
        count = (last - first) * per
        spread = one_hot(iota((count, last - first), 0) // per == iota((count, last - first), 1))
        got = dot(spread, asked[first:last].reshape(last - first, 128).astype(BF))
        lanes = iota((count, 128), 1)
        turn = iota((count, 128), 0) % per
        want = jnp.sum(
            jnp.where(lanes == turn, got * 8.0, jnp.where(lanes == turn + per, got, 0.0)), axis=1, keepdims=True
        ).astype(jnp.int32)
        rows = dot(one_hot(iota((count, shard), 1) == want), cold_ref[...])
        base = first * per * pieces
        for j in range(pieces):
            wide[pl.ds(base + j, count, stride=pieces), :] = rows[:, j * 128 : (j + 1) * 128]
        found[first:last] = (
            wide[base : base + count * pieces].astype(BF).reshape(last - first, per * pieces, 128)
        )
        send(found, reply, low_d, high_d, reply_send, reply_recv)
        if k == 0:
            reply[core] = found[core]
    take = one_hot(iota((tokens, tokens), 1) == jnp.where(cold, owner * per + place, -1))
    meanwhile()
    settle(reply, 1, n, reply_recv)

    wide[...] = reply[...].reshape(wide.shape).astype(F32)
    for j in range(pieces):
        cut = slice(j * 128, (j + 1) * 128)
        piece = wide[pl.ds(j, tokens, stride=pieces), :].astype(BF)
        emb_ref[:, cut] += dot(take, piece)

    def end():
        settle(ask, 1, n, ask_send)
        settle(found, 1, n, reply_send)

    return end


def normalised(values):
    mean = jnp.mean(values, axis=-1, keepdims=True)
    centred = values - mean
    scale = lax.rsqrt(jnp.mean(centred * centred, axis=-1, keepdims=True) + 1e-05)
    return centred * scale, scale


def silu_both(v):
    sig = 0.5 * jnp.tanh(0.5 * v) + 0.5
    act = v * sig
    return act, sig + act * (1.0 - sig)


CHUNKS = 5
WIDE = 256


class Ring:
    def __init__(self, g, in1, out1, total, tot_bf, in2, out2, send1, recv1, send2, recv2):
        self.g, self.in1, self.out1, self.total, self.tot_bf = g, in1, out1, total, tot_bf
        self.in2, self.out2 = in2, out2
        self.sems = ((send1, recv1), (send2, recv2))
        me = lax.axis_index("bal")
        x, y = me // 4, me % 4
        self.places = ((x, y), (y, x))
        along_x = tuple((x + step) % 4 * 4 + y for step in (1, 3))
        along_y = tuple(x * 4 + (y + step) % 4 for step in (1, 3))
        self.peers = ((along_x, along_y), (along_y, along_x))
        self.near = (*along_x, *along_y)
        self.sent = {}

    def post(self, stage, c, half, way, msg):
        at = self.places[half][stage]
        step = (1, 3)[way]
        if stage == 0:
            mine, other = pl.ds(2 * way, 2), pl.ds(2 - 2 * way, 2)
            src, land, out = self.g, self.in1, self.out1
        else:
            mid = self.tot_bf.shape[3] // 2
            mine, other = pl.ds(mid * way, mid), pl.ds(mid - mid * way, mid)
            src, land, out = self.tot_bf, self.in2, self.out2
        ref = (
            src.at[c, half, (at + 2) % 4, mine],
            src.at[c, half, (at + step) % 4, other],
            out.at[c, half, way],
        )[msg]
        send, recv = self.sems[stage]
        copy = pltpu.make_async_remote_copy(
            src_ref=ref, dst_ref=land.at[c, half, way, msg],
            send_sem=send.at[c, half, way, msg], recv_sem=recv.at[c, half, way, msg],
            device_id={"bal": self.peers[half][stage][way]}, device_id_type=pl.DeviceIdType.MESH,
        )
        copy.start()
        self.sent[stage, c, half, way, msg] = copy

    def arrive(self, stage, c, half, way, msg):
        self.sent[stage, c, half, way, msg].wait_recv()

    def start(self, stage, c):
        for msg in (0, 1):
            for half in range(2):
                for way in range(2):
                    self.post(stage, c, half, way, msg)

    def relay(self, stage, c):
        for half in range(2):
            at = self.places[half][stage]
            for way in range(2):
                self.arrive(stage, c, half, way, 0)
                to = (at + (1, 3)[way]) % 4
                if stage == 0:
                    own = self.g[c, half, to, pl.ds(2 * way, 2)].astype(F32)
                    self.out1[c, half, way] = (own + self.in1[c, half, way, 0].astype(F32)).astype(BF)
                else:
                    mid = self.tot_bf.shape[3] // 2
                    own = self.total[c, half, to, pl.ds(mid * way, mid)]
                    self.out2[c, half, way] = (own + self.in2[c, half, way, 0].astype(F32)).astype(BF)
                self.post(stage, c, half, way, 2)

    def turn(self, c):
        for half in range(2):
            a = self.places[half][0]
            for way in range(2):
                self.arrive(0, c, half, way, 1)
                self.arrive(0, c, half, way, 2)
            for part in range(2):
                here = pl.ds(2 * part, 2)
                t = (
                    self.g[c, half, a, here].astype(F32)
                    + self.in1[c, half, part, 2].astype(F32)
                    + self.in1[c, half, 1 - part, 1].astype(F32)
                )
                self.total[c, half, here] = t
                self.tot_bf[c, half, here] = t.astype(BF)
        self.start(1, c)

    def finish(self, c, store):
        mid = self.tot_bf.shape[3] // 2
        for half in range(2):
            b = self.places[half][1]
            for way in range(2):
                self.arrive(1, c, half, way, 1)
                self.arrive(1, c, half, way, 2)
            for part in range(2):
                rows = pl.ds(mid * part, mid)
                store(
                    c, half, rows,
                    self.total[c, half, b, rows]
                    + self.in2[c, half, part, 2].astype(F32)
                    + self.in2[c, half, 1 - part, 1].astype(F32),
                )

    def drain(self):
        for copy in self.sent.values():
            copy.wait_send()


def layer_kernel(
    n_table, grad_scale, ids_hbm, len_hbm, slot_hbm, hot_hbm, cold_hbm, cot_hbm, wu_hbm, wo_hbm,
    out_ref, first_ref, second_ref,
    ids_ref, len_ref, slot_ref, hot_ref, cold_ref, cot_ref, wu_ref, wo_ref, ask, asked, wide, found, reply, emb_ref,
    slope, acts, attn, attn_slope, mixed, grads, signal_ref, back_ref,
    load_sem, ask_send, ask_recv, reply_send, reply_recv, *ring_refs,
):
    tokens, features = emb_ref.shape
    loads = [
        pltpu.make_async_copy(src, dst, load_sem.at[k])
        for k, (src, dst) in enumerate((
            (slot_hbm, slot_ref), (cold_hbm, cold_ref), (hot_hbm, hot_ref),
            (cot_hbm, cot_ref), (wo_hbm, wo_ref), (wu_hbm, wu_ref), (ids_hbm, ids_ref), (len_hbm, len_ref),
        ))
    ]
    for k in (6, 7, 0, 1, 2, 3, 4, 5):
        loads[k].start()
    ring = Ring(*ring_refs)
    users = tokens // MAXLEN
    head = features // HEADS
    first = (lax.axis_index("table") * lax.axis_size("bal") + lax.axis_index("bal")) * users

    def valid_below():
        return [len_ref[first + u] for u in range(users)]

    def cotangent():
        for load in loads[3:6] + loads[7:]:
            load.wait()
        lengths = valid_below()
        at = iota((tokens, 1), 0)
        ends = jnp.full((tokens, 1), lengths[0], jnp.int32)
        for u in range(1, users):
            ends = jnp.where(at >= u * MAXLEN, u * MAXLEN + lengths[u], ends)
        signal = (jnp.where(at < ends, cot_ref[...].astype(F32), 0.0) * grad_scale).astype(BF)
        signal_ref[...] = signal
        back_ref[...] = dot(signal, wo_ref[...], 1, 1).astype(BF)

    end = lookup(
        n_table, loads, ring.near, cotangent, ids_ref, slot_ref, hot_ref, cold_ref, ask, asked, wide, found, reply,
        emb_ref, ask_send, ask_recv, reply_send, reply_recv,
    )
    emb = emb_ref[...]
    normed = normalised(emb)[0].astype(BF)
    for b in (2, 3, 1, 0):
        cut = slice(b * features, (b + 1) * features)
        act, dact = silu_both(dot(normed, wu_ref[:, cut]))
        acts[:, cut] = act.astype(BF)
        slope[:, cut] = dact
    lengths = valid_below()
    i, j = iota((MAXLEN, MAXLEN), 0), iota((MAXLEN, MAXLEN), 1)
    scale = 1.0 / math.sqrt(head)

    def part(b, u, h):
        at = b * features + h * head
        return acts[u * MAXLEN : (u + 1) * MAXLEN, at : at + head]

    for u in range(users):
        allowed = (j <= i) & (i < lengths[u])
        for h in range(HEADS):
            s = dot(part(2, u, h), part(3, u, h), 1, 1) * scale
            act, dact = silu_both(s)
            w = jnp.where(allowed, act, 0.0).astype(BF)
            attn[u * HEADS + h] = w
            attn_slope[u * HEADS + h] = jnp.where(allowed, dact * scale, 0.0)
            mixed[u * MAXLEN : (u + 1) * MAXLEN, h * head : (h + 1) * head] = dot(w, part(1, u, h))

    n, rstd = normalised(mixed[...])
    gate = acts[:, :features].astype(F32)
    gated = (n * gate).astype(BF)
    signal = signal_ref[...]

    def spread(c, left, right):
        for half in range(2):
            value = dot(left, right[:, half * WIDE : (half + 1) * WIDE], 0, 0).astype(BF)
            height = features // 16
            for b in range(16):
                x, y = divmod(b, 4)
                f, s = (x, y) if half == 0 else (y, x)
                ring.g[c, half, f, s] = value[b * height : (b + 1) * height]
        ring.start(0, c)

    spread(0, gated, signal)
    back = back_ref[...].astype(F32)
    grads[:, :features] = ((back * n).astype(BF).astype(F32) * slope[:, :features]).astype(BF)
    spread(1, normed, grads[:, :features])
    dn = back * gate
    mixed[...] = rstd * (
        dn - jnp.mean(dn, axis=-1, keepdims=True) - n * jnp.mean(dn * n, axis=-1, keepdims=True)
    )
    for u in range(users):
        rows = slice(u * MAXLEN, (u + 1) * MAXLEN)
        for h in range(HEADS):
            dm = mixed[rows, h * head : (h + 1) * head].astype(BF)
            w = attn[u * HEADS + h]
            dw = dot(dm, part(1, u, h), 1, 1).astype(BF).astype(F32)
            ds = (dw * attn_slope[u * HEADS + h]).astype(BF)
            for b, d in (
                (1, dot(w, dm, 0, 0)),
                (2, dot(ds, part(3, u, h))),
                (3, dot(ds, part(2, u, h), 0, 0)),
            ):
                cols = slice(b * features + h * head, b * features + (h + 1) * head)
                grads[rows, cols] = (d.astype(BF).astype(F32) * slope[rows, cols]).astype(BF)
    ring.relay(0, 0)
    spread(2, normed, grads[:, features : 2 * features])
    ring.relay(0, 1)
    spread(3, normed, grads[:, 2 * features : 3 * features])
    spread(4, normed, grads[:, 3 * features :])
    ring.relay(0, 2)
    ring.turn(0)
    ring.relay(0, 3)
    ring.turn(1)
    out_ref[...] = (emb + dot(gated, wo_ref[...])).astype(BF)
    ring.relay(0, 4)
    ring.relay(1, 0)
    ring.turn(2)
    ring.relay(1, 1)
    ring.turn(3)

    def store(c, half, rows, value):
        if c == 0:
            second_ref[rows, half * WIDE : (half + 1) * WIDE] = value
        else:
            low = (c - 1) * features + half * WIDE
            first_ref[rows, low : low + WIDE] = value

    ring.relay(1, 2)
    ring.finish(0, store)
    ring.turn(4)
    ring.relay(1, 3)
    ring.finish(1, store)
    ring.finish(2, store)
    ring.relay(1, 4)
    ring.finish(3, store)
    ring.finish(4, store)
    ring.drain()
    end()


def ring_scratch(height):
    dma = pltpu.SemaphoreType.DMA((CHUNKS, 2, 2, 3))
    return [
        pltpu.VMEM((CHUNKS, 2, 4, 4, height, WIDE), BF),
        pltpu.VMEM((CHUNKS, 2, 2, 3, 2, height, WIDE), BF),
        pltpu.VMEM((CHUNKS, 2, 2, 2, height, WIDE), BF),
        pltpu.VMEM((CHUNKS, 2, 4, height, WIDE), F32),
        pltpu.VMEM((CHUNKS, 2, 4, height, WIDE), BF),
        pltpu.VMEM((CHUNKS, 2, 2, 3, height // 2, WIDE), BF),
        pltpu.VMEM((CHUNKS, 2, 2, height // 2, WIDE), BF),
        dma, dma, dma, dma,
    ]


def layer(n, grad_scale, ids, hot_slot, hot_rows, cold_rows, lengths, cot, wu, wo):
    tokens, features = cot.shape
    users = tokens // MAXLEN
    height = features // 16
    piece = features // 128 * (tokens // n)
    lines = hot_slot.reshape(-1, 128)
    return pl.pallas_call(
        functools.partial(layer_kernel, n, grad_scale),
        out_shape=(
            jax.ShapeDtypeStruct((tokens, features), BF),
            jax.ShapeDtypeStruct((height, 4 * features), F32),
            jax.ShapeDtypeStruct((height, features), F32),
        ),
        in_specs=[HBM] * 8,
        out_specs=(VMEM, VMEM, VMEM),
        scratch_shapes=[
            pltpu.VMEM((1, tokens), jnp.int32),
            pltpu.SMEM(lengths.shape, jnp.int32),
            pltpu.VMEM(lines.shape, jnp.int32),
            pltpu.VMEM(hot_rows.shape, BF),
            pltpu.VMEM(cold_rows.shape, BF),
            pltpu.VMEM(cot.shape, BF),
            pltpu.VMEM(wu.shape, BF),
            pltpu.VMEM(wo.shape, BF),
            pltpu.VMEM((n, 1, 128), F32),
            pltpu.VMEM((n, 1, 128), F32),
            pltpu.VMEM((n * piece, 128), F32),
            pltpu.VMEM((n, piece, 128), BF),
            pltpu.VMEM((n, piece, 128), BF),
            pltpu.VMEM((tokens, features), F32),
            pltpu.VMEM((tokens, 4 * features), F32),
            pltpu.VMEM((tokens, 4 * features), BF),
            pltpu.VMEM((users * HEADS, MAXLEN, MAXLEN), BF),
            pltpu.VMEM((users * HEADS, MAXLEN, MAXLEN), F32),
            pltpu.VMEM((tokens, features), F32),
            pltpu.VMEM((tokens, 4 * features), BF),
            pltpu.VMEM((tokens, features), BF),
            pltpu.VMEM((tokens, features), BF),
            pltpu.SemaphoreType.DMA((8,)),
            pltpu.SemaphoreType.DMA,
            pltpu.SemaphoreType.DMA((4,)),
            pltpu.SemaphoreType.DMA,
            pltpu.SemaphoreType.DMA,
            *ring_scratch(height),
        ],
        compiler_params=pltpu.CompilerParams(
            collective_id=0, has_side_effects=True, vmem_limit_bytes=36 * 2**20
        ),
        name="layer",
    )(
        *(
            pltpu.with_memory_space_constraint(a, pltpu.HBM)
            for a in (ids.reshape(1, tokens), lengths, lines, hot_rows, cold_rows, cot, wu, wo)
        ),
    )


def per_device(item_ids, hot_slot, hot_rows, cold_rows, hist_lengths, out_grad, w_uvqk, w_out):
    grad_scale = 1.0 / math.sqrt(lax.axis_size("bal") * out_grad.shape[0])
    return layer(
        lax.axis_size("table"), grad_scale, item_ids, hot_slot, hot_rows, cold_rows, hist_lengths, out_grad, w_uvqk, w_out
    )


def solution(mesh):
    both = P(("table", "bal"), None)
    return jax.shard_map(
        per_device,
        mesh=mesh,
        in_specs=(P(("table", "bal")), P(), P(), P("table", None), P(), both, P(), P()),
        out_specs=(both, both, both),
        check_vma=False,
    )
```

time: 291 us -> 96.2 us (0.33)
  waiting for transfers between devices: 143 us -> 0 us
  Pallas kernels: 0 us -> 93.2 us
  blocking collectives: 52.7 us -> 0 us
  local copies, waits for them, and re-layouts: 30.1 us -> 2.04 us
  other arithmetic: 27 us -> 0 us
  matrix products: 17.2 us -> 0 us
  between operations: 14.2 us -> 0.64 us
  starting transfers between devices: 4.85 us -> 0 us
    reduce_scatter x1 -> x0, waiting for transfers between devices: 102 us -> none  [side_by_side(): lax.psum_scatter(both, axis, scatter_dimension=dim, tiled=True)]
    pallas_call x0 -> x1, Pallas kernels: none -> 93.2 us  [layer(): pl.pallas_call(functools.partial(layer_kernel, n, grad_scale), out_shape=...]
    all_to_all x1 -> x0, blocking collectives: 52.7 us -> none  [per_device(): lax.all_to_all(requests, 'table', split_axis=0, concat_axis=0, tiled=True)]
    all_to_all x1 -> x0, waiting for transfers between devices: 41.1 us -> none  [per_device(): lax.all_to_all(found_rows, 'table', split_axis=0, concat_axis=0, tiled=True)]
    dot_general x22 -> x0, matrix products: 17.2 us -> none  [the longest x2 6.78 us: user_pass(): jnp.einsum('td,tf->df', normed, grad_hidden, preferred_element_type=jnp.f...]
    add x4 -> x0, other arithmetic: 13 us -> none  [per_user(): return ((running[0] + grad_first, running[1] + grad_second), output)]
    scatter x1 -> x0, local copies, waits for them, and re-layouts: 11.3 us -> none  [per_device(): jnp.zeros((owners, capacity), jnp.int32).at[target, position]]
    gather x5 -> x0, local copies, waits for them, and re-layouts: 6.66 us -> none  [the longest x1 2.19 us: per_device(): hot_index = jnp.take(hot_slot, item_ids)]
  transfers between devices with their start and end apart: 2 -> 0, of which waited for: 2 -> 0; matrix products, arithmetic and copies ran while one was open for 1% -> 0% of each run, Pallas kernels for 0% -> 0%
where the time goes in v2:
time: 96.2 us; the launch traced here: 95.9 us
  Pallas kernels  93.2 us (97%)
  local copies, waits for them, and re-layouts  2.04 us (2%)
    pallas_call x1, Pallas kernels, layer(): pl.pallas_call(functools.partial(layer_kernel, n, grad_scale), out_shape=...  93.2 us
    unnamed x3, local copies, waits for them, and re-layouts  2.04 us

profile of v2, /device:TPU:6, one launch (start us, length us, event | category | flops | bytes accessed | tf_op | source)
XLA Modules:
  0.0 95.9 jit_solution(16226341082087122437)
XLA Ops:
  0.6 93.2 %layer.1 = (bf16[256,512]{1,0:T(8,128)(2,1)S(1)}, f32[32,2048]{1,0:T(8,128)S(1)}, f32[32,512]{1,0:T(8,128)S(1)}) custom-call(s32[1,256]{1,0:T(1,128)} %bitcast.3, s32[2048]{0:T(1024)} %len_hbm.1, s32[512,128]{1,0:T(8,128)} %bitcast.2, bf16[1024,512]{1,0:T(8,128)(2,1)} %hot_hbm.1, bf16[1024,512]{1,0:T(8,128)(2,1)} %cold_hbm.1, bf16[256,512]{1,0:T(8,128)(2,1)} %cot_hbm.1, ...), custom_call_target="tpu_custom_call" | custom-call | tf_op jit(solution)/shard_map/layer/pallas_call | solution.py:447
  93.9 0.7 copy.14
  94.6 0.7 copy.15
  95.3 0.6 copy.16

commit v3 on v2

--- a/solution.py
+++ b/solution.py
@@ -181,14 +181,16 @@
     return act, sig + act * (1.0 - sig)
 
 
-CHUNKS = 5
 WIDE = 256
+GROUPS = ((4, 0), (1, 2, 3))
 
 
 class Ring:
-    def __init__(self, g, in1, out1, total, tot_bf, in2, out2, send1, recv1, send2, recv2):
-        self.g, self.in1, self.out1, self.total, self.tot_bf = g, in1, out1, total, tot_bf
-        self.in2, self.out2 = in2, out2
+    def __init__(self, send1, recv1, send2, recv2, *refs):
+        count = len(GROUPS)
+        self.g, self.in1, self.out1, self.total, self.tot_bf, self.in2, self.out2 = (
+            refs[k * count : (k + 1) * count] for k in range(7)
+        )
         self.sems = ((send1, recv1), (send2, recv2))
         me = lax.axis_index("bal")
         x, y = me // 4, me % 4
@@ -206,17 +208,17 @@
             mine, other = pl.ds(2 * way, 2), pl.ds(2 - 2 * way, 2)
             src, land, out = self.g, self.in1, self.out1
         else:
-            mid = self.tot_bf.shape[3] // 2
+            mid = self.tot_bf[c].shape[2] // 2
             mine, other = pl.ds(mid * way, mid), pl.ds(mid - mid * way, mid)
             src, land, out = self.tot_bf, self.in2, self.out2
         ref = (
-            src.at[c, half, (at + 2) % 4, mine],
-            src.at[c, half, (at + step) % 4, other],
-            out.at[c, half, way],
+            src[c].at[half, (at + 2) % 4, mine],
+            src[c].at[half, (at + step) % 4, other],
+            out[c].at[half, way],
         )[msg]
         send, recv = self.sems[stage]
         copy = pltpu.make_async_remote_copy(
-            src_ref=ref, dst_ref=land.at[c, half, way, msg],
+            src_ref=ref, dst_ref=land[c].at[half, way, msg],
             send_sem=send.at[c, half, way, msg], recv_sem=recv.at[c, half, way, msg],
             device_id={"bal": self.peers[half][stage][way]}, device_id_type=pl.DeviceIdType.MESH,
         )
@@ -239,12 +241,12 @@
                 self.arrive(stage, c, half, way, 0)
                 to = (at + (1, 3)[way]) % 4
                 if stage == 0:
-                    own = self.g[c, half, to, pl.ds(2 * way, 2)].astype(F32)
-                    self.out1[c, half, way] = (own + self.in1[c, half, way, 0].astype(F32)).astype(BF)
+                    own = self.g[c][half, to, pl.ds(2 * way, 2)].astype(F32)
+                    self.out1[c][half, way] = (own + self.in1[c][half, way, 0].astype(F32)).astype(BF)
                 else:
-                    mid = self.tot_bf.shape[3] // 2
-                    own = self.total[c, half, to, pl.ds(mid * way, mid)]
-                    self.out2[c, half, way] = (own + self.in2[c, half, way, 0].astype(F32)).astype(BF)
+                    mid = self.tot_bf[c].shape[2] // 2
+                    own = self.total[c][half, to, pl.ds(mid * way, mid)]
+                    self.out2[c][half, way] = (own + self.in2[c][half, way, 0].astype(F32)).astype(BF)
                 self.post(stage, c, half, way, 2)
 
     def turn(self, c):
@@ -256,16 +258,16 @@
             for part in range(2):
                 here = pl.ds(2 * part, 2)
                 t = (
-                    self.g[c, half, a, here].astype(F32)
-                    + self.in1[c, half, part, 2].astype(F32)
-                    + self.in1[c, half, 1 - part, 1].astype(F32)
+                    self.g[c][half, a, here].astype(F32)
+                    + self.in1[c][half, part, 2].astype(F32)
+                    + self.in1[c][half, 1 - part, 1].astype(F32)
                 )
-                self.total[c, half, here] = t
-                self.tot_bf[c, half, here] = t.astype(BF)
+                self.total[c][half, here] = t
+                self.tot_bf[c][half, here] = t.astype(BF)
         self.start(1, c)
 
     def finish(self, c, store):
-        mid = self.tot_bf.shape[3] // 2
+        mid = self.tot_bf[c].shape[2] // 2
         for half in range(2):
             b = self.places[half][1]
             for way in range(2):
@@ -275,9 +277,9 @@
                 rows = pl.ds(mid * part, mid)
                 store(
                     c, half, rows,
-                    self.total[c, half, b, rows]
-                    + self.in2[c, half, part, 2].astype(F32)
-                    + self.in2[c, half, 1 - part, 1].astype(F32),
+                    self.total[c][half, b, rows]
+                    + self.in2[c][half, part, 2].astype(F32)
+                    + self.in2[c][half, 1 - part, 1].astype(F32),
                 )
 
     def drain(self):
@@ -356,20 +358,23 @@
     gated = (n * gate).astype(BF)
     signal = signal_ref[...]
 
-    def spread(c, left, right):
+    def spread(block, left, right):
+        [c] = [c for c, group in enumerate(GROUPS) if block in group]
+        at = GROUPS[c].index(block) * WIDE
+        height = features // 16
         for half in range(2):
             value = dot(left, right[:, half * WIDE : (half + 1) * WIDE], 0, 0).astype(BF)
-            height = features // 16
             for b in range(16):
                 x, y = divmod(b, 4)
                 f, s = (x, y) if half == 0 else (y, x)
-                ring.g[c, half, f, s] = value[b * height : (b + 1) * height]
-        ring.start(0, c)
-
-    spread(0, gated, signal)
+                ring.g[c][half, f, s, :, at : at + WIDE] = value[b * height : (b + 1) * height]
+        if block == GROUPS[c][-1]:
+            ring.start(0, c)
+
+    spread(4, gated, signal)
     back = back_ref[...].astype(F32)
     grads[:, :features] = ((back * n).astype(BF).astype(F32) * slope[:, :features]).astype(BF)
-    spread(1, normed, grads[:, :features])
+    spread(0, normed, grads[:, :features])
     dn = back * gate
     mixed[...] = rstd * (
         dn - jnp.mean(dn, axis=-1, keepdims=True) - n * jnp.mean(dn * n, axis=-1, keepdims=True)
@@ -388,53 +393,45 @@
             ):
                 cols = slice(b * features + h * head, b * features + (h + 1) * head)
                 grads[rows, cols] = (d.astype(BF).astype(F32) * slope[rows, cols]).astype(BF)
-    ring.relay(0, 0)
-    spread(2, normed, grads[:, features : 2 * features])
-    ring.relay(0, 1)
-    spread(3, normed, grads[:, 2 * features : 3 * features])
-    spread(4, normed, grads[:, 3 * features :])
-    ring.relay(0, 2)
-    ring.turn(0)
-    ring.relay(0, 3)
-    ring.turn(1)
+    for b in range(1, 4):
+        spread(b, normed, grads[:, b * features : (b + 1) * features])
+
+    def store(c, half, rows, value):
+        for k, block in enumerate(GROUPS[c]):
+            piece = value[:, k * WIDE : (k + 1) * WIDE]
+            low = half * WIDE
+            if block == 4:
+                second_ref[rows, low : low + WIDE] = piece
+            else:
+                first_ref[rows, block * features + low : block * features + low + WIDE] = piece
+
+    chunks = range(len(GROUPS))
+    for c in chunks:
+        ring.relay(0, c)
     out_ref[...] = (emb + dot(gated, wo_ref[...])).astype(BF)
-    ring.relay(0, 4)
-    ring.relay(1, 0)
-    ring.turn(2)
-    ring.relay(1, 1)
-    ring.turn(3)
-
-    def store(c, half, rows, value):
-        if c == 0:
-            second_ref[rows, half * WIDE : (half + 1) * WIDE] = value
-        else:
-            low = (c - 1) * features + half * WIDE
-            first_ref[rows, low : low + WIDE] = value
-
-    ring.relay(1, 2)
-    ring.finish(0, store)
-    ring.turn(4)
-    ring.relay(1, 3)
-    ring.finish(1, store)
-    ring.finish(2, store)
-    ring.relay(1, 4)
-    ring.finish(3, store)
-    ring.finish(4, store)
+    for c in chunks:
+        ring.turn(c)
+    for c in chunks:
+        ring.relay(1, c)
+    for c in chunks:
+        ring.finish(c, store)
     ring.drain()
     end()
 
 
 def ring_scratch(height):
-    dma = pltpu.SemaphoreType.DMA((CHUNKS, 2, 2, 3))
-    return [
-        pltpu.VMEM((CHUNKS, 2, 4, 4, height, WIDE), BF),
-        pltpu.VMEM((CHUNKS, 2, 2, 3, 2, height, WIDE), BF),
-        pltpu.VMEM((CHUNKS, 2, 2, 2, height, WIDE), BF),
-        pltpu.VMEM((CHUNKS, 2, 4, height, WIDE), F32),
-        pltpu.VMEM((CHUNKS, 2, 4, height, WIDE), BF),
-        pltpu.VMEM((CHUNKS, 2, 2, 3, height // 2, WIDE), BF),
-        pltpu.VMEM((CHUNKS, 2, 2, height // 2, WIDE), BF),
-        dma, dma, dma, dma,
+    dma = pltpu.SemaphoreType.DMA((len(GROUPS), 2, 2, 3))
+    shapes = (
+        ((2, 4, 4, height), BF),
+        ((2, 2, 3, 2, height), BF),
+        ((2, 2, 2, height), BF),
+        ((2, 4, height), F32),
+        ((2, 4, height), BF),
+        ((2, 2, 3, height // 2), BF),
+        ((2, 2, height // 2), BF),
+    )
+    return [dma] * 4 + [
+        pltpu.VMEM((*shape, WIDE * len(group)), kind) for shape, kind in shapes for group in GROUPS
     ]
 
 

time: 96.2 us -> 92.2 us (0.958)
  Pallas kernels: 93.2 us -> 89.3 us
    pallas_call x1, Pallas kernels: 93.2 us -> 89.3 us  [layer(): pl.pallas_call(functools.partial(layer_kernel, n, grad_scale), out_shape=...]
where the time goes in v3:
time: 92.2 us; the launch traced here: 92 us
  Pallas kernels  89.3 us (97%)
  local copies, waits for them, and re-layouts  2.04 us (2%)
    pallas_call x1, Pallas kernels, layer(): pl.pallas_call(functools.partial(layer_kernel, n, grad_scale), out_shape=...  89.3 us
    unnamed x3, local copies, waits for them, and re-layouts  2.04 us

profile of v3, /device:TPU:6, one launch (start us, length us, event | category | flops | bytes accessed | tf_op | source)
XLA Modules:
  0.0 92.0 jit_solution(11590539008814246443)
XLA Ops:
  0.6 89.3 %layer.1 = (bf16[256,512]{1,0:T(8,128)(2,1)S(1)}, f32[32,2048]{1,0:T(8,128)S(1)}, f32[32,512]{1,0:T(8,128)S(1)}) custom-call(s32[1,256]{1,0:T(1,128)} %bitcast.3, s32[2048]{0:T(1024)} %len_hbm.1, s32[512,128]{1,0:T(8,128)} %bitcast.2, bf16[1024,512]{1,0:T(8,128)(2,1)} %hot_hbm.1, bf16[1024,512]{1,0:T(8,128)(2,1)} %cold_hbm.1, bf16[256,512]{1,0:T(8,128)(2,1)} %cot_hbm.1, ...), custom_call_target="tpu_custom_call" | custom-call | tf_op jit(solution)/shard_map/layer/pallas_call | solution.py:444
  89.9 0.7 copy.14
  90.6 0.7 copy.15
  91.3 0.6 copy.16

commit v4 on v3

--- a/solution.py
+++ b/solution.py
@@ -492,11 +492,31 @@
     )
 
 
+def put_kernel(*refs):
+    count = len(refs) // 2
+    copies = [pltpu.make_async_copy(refs[k], refs[count + k], refs[-1].at[k]) for k in range(count)]
+    for copy in copies:
+        copy.start()
+    for copy in copies:
+        copy.wait()
+
+
+def put(*arrays):
+    return pl.pallas_call(
+        put_kernel,
+        out_shape=tuple(jax.ShapeDtypeStruct(a.shape, a.dtype) for a in arrays),
+        in_specs=[VMEM] * len(arrays),
+        out_specs=(HBM,) * len(arrays),
+        scratch_shapes=[pltpu.SemaphoreType.DMA((len(arrays),))],
+        name="put",
+    )(*(pltpu.with_memory_space_constraint(a, pltpu.VMEM) for a in arrays))
+
+
 def per_device(item_ids, hot_slot, hot_rows, cold_rows, hist_lengths, out_grad, w_uvqk, w_out):
     grad_scale = 1.0 / math.sqrt(lax.axis_size("bal") * out_grad.shape[0])
-    return layer(
+    return put(*layer(
         lax.axis_size("table"), grad_scale, item_ids, hot_slot, hot_rows, cold_rows, hist_lengths, out_grad, w_uvqk, w_out
-    )
+    ))
 
 
 def solution(mesh):

time: 92.2 us -> 91 us (0.987)
  local copies, waits for them, and re-layouts: 2.04 us -> 0 us
    unnamed x3 -> x0, local copies, waits for them, and re-layouts: 2.04 us -> none
where the time goes in v4:
time: 91 us; the launch traced here: 90.8 us
  Pallas kernels  90.1 us (99%)
    pallas_call x1, Pallas kernels, layer(): pl.pallas_call(functools.partial(layer_kernel, n, grad_scale), out_shape=...  89.3 us

profile of v4, /device:TPU:6, one launch (start us, length us, event | category | flops | bytes accessed | tf_op | source)
XLA Modules:
  0.0 90.8 jit_solution(8336550392734996633)
XLA Ops:
  0.6 89.3 %layer.1 = (bf16[256,512]{1,0:T(8,128)(2,1)S(1)}, f32[32,2048]{1,0:T(8,128)S(1)}, f32[32,512]{1,0:T(8,128)S(1)}) custom-call(s32[1,256]{1,0:T(1,128)} %bitcast.3, s32[2048]{0:T(1024)} %len_hbm.1, s32[512,128]{1,0:T(8,128)} %bitcast.2, bf16[1024,512]{1,0:T(8,128)(2,1)} %hot_hbm.1, bf16[1024,512]{1,0:T(8,128)(2,1)} %cold_hbm.1, bf16[256,512]{1,0:T(8,128)(2,1)} %cot_hbm.1, ...), custom_call_target="tpu_custom_call" | custom-call | tf_op jit(solution)/shard_map/layer/pallas_call | solution.py:444
  89.9 0.8 put.1

commit v5 on v4

--- a/solution.py
+++ b/solution.py
@@ -282,9 +282,10 @@
                     + self.in2[c][half, 1 - part, 1].astype(F32),
                 )
 
-    def drain(self):
-        for copy in self.sent.values():
-            copy.wait_send()
+    def drain(self, stage):
+        for key, copy in self.sent.items():
+            if key[0] == stage:
+                copy.wait_send()
 
 
 def layer_kernel(
@@ -411,12 +412,13 @@
     out_ref[...] = (emb + dot(gated, wo_ref[...])).astype(BF)
     for c in chunks:
         ring.turn(c)
+    ring.drain(0)
+    end()
     for c in chunks:
         ring.relay(1, c)
     for c in chunks:
         ring.finish(c, store)
-    ring.drain()
-    end()
+    ring.drain(1)
 
 
 def ring_scratch(height):

time: 91 us -> 90.9 us (level)
  no operation moved by 1% of the time
where the time goes in v5:
time: 90.9 us; the launch traced here: 90.7 us
  Pallas kernels  90.1 us (99%)
    pallas_call x1, Pallas kernels, layer(): pl.pallas_call(functools.partial(layer_kernel, n, grad_scale), out_shape=...  89.3 us

profile of v5, /device:TPU:6, one launch (start us, length us, event | category | flops | bytes accessed | tf_op | source)
XLA Modules:
  0.0 90.7 jit_solution(1279892053335554828)
XLA Ops:
  0.6 89.3 %layer.1 = (bf16[256,512]{1,0:T(8,128)(2,1)S(1)}, f32[32,2048]{1,0:T(8,128)S(1)}, f32[32,512]{1,0:T(8,128)S(1)}) custom-call(s32[1,256]{1,0:T(1,128)} %bitcast.3, s32[2048]{0:T(1024)} %len_hbm.1, s32[512,128]{1,0:T(8,128)} %bitcast.2, bf16[1024,512]{1,0:T(8,128)(2,1)} %hot_hbm.1, bf16[1024,512]{1,0:T(8,128)(2,1)} %cold_hbm.1, bf16[256,512]{1,0:T(8,128)(2,1)} %cot_hbm.1, ...), custom_call_target="tpu_custom_call" | custom-call | tf_op jit(solution)/shard_map/layer/pallas_call | solution.py:446
  89.9 0.8 put.1
